TPU v7x, 512 devices: a whole 4x4x16 slice. The times are simulated.
512 devices in a mesh: seq: 128 (over z, x, core), batch: 4 (over y).
Axes of the slice: x: 4, y: 4, z: 16, core: 2. Of those that a mesh axis runs over, the one named last changes fastest.
Arguments:
- tokens: bfloat16 [4, 128, 128, 1152], P('batch', 'seq'), may hold values from -6 to 6
- spatial_query: bfloat16 [4, 128, 128, 1152], P('batch', 'seq'), may hold values from -24 to 24
- spatial_key: bfloat16 [4, 128, 128, 1152], P('batch', 'seq'), may hold values from -24 to 24
- spatial_value: bfloat16 [4, 128, 128, 1152], P('batch', 'seq'), may hold values from -6 to 6
- frame_counts: int32 [4, 16], P('batch'), may hold values from 1 to 64, 128 in all within a row
- w_spatial_out: bfloat16 [1152, 1152], P('seq', 'batch'), may hold values from -0.1875 to 0.1875
- w_temporal_qkv: bfloat16 [1152, 3456], P('seq', 'batch'), may hold values from -3 to 3
- w_temporal_out: bfloat16 [1152, 1152], P('seq', 'batch'), may hold values from -0.1875 to 0.1875
Outputs:
- block_out: bfloat16 [4, 128, 128, 1152], P('batch', 'seq')
Inputs may be any that keep to these rules, and one draw needn't show every extreme that they name: `frame_counts`: the counts of a group sum to 128; one clip has exactly 64 frames.
All inputs are finite; a program needn't handle non-finite values.
Results may differ from a plain program's by a relative error of at most 0.015.
Values may be sent and summed in bfloat16 or wider, within the bound.
A program may use at most 128 MiB of HBM per device.

v0:
```python
import jax
import jax.numpy as jnp
from jax import lax
from jax.sharding import PartitionSpec as P

HEADS = 16


EPS = 1e-06


def fold_rows(left, piece):
    return jnp.dot(left, piece, preferred_element_type=jnp.float32)


def layer_norm(hidden):
    wide = hidden.astype(jnp.float32)
    mean = jnp.mean(wide, axis=1, keepdims=True)
    var = jnp.mean((wide - mean) ** 2, axis=1, keepdims=True)
    return ((wide - mean) * lax.rsqrt(var + EPS)).astype(jnp.bfloat16)


def temporal_attention(t_query, t_key, t_value, same):
    frames, part, width = t_query.shape
    shape = (frames, part, HEADS, width // HEADS)
    scale = 1.0 / jnp.sqrt(jnp.float32(width // HEADS))
    scores = (
        jnp.einsum(
            "fphd,gphd->phfg",
            t_query.reshape(shape),
            t_key.reshape(shape),
            preferred_element_type=jnp.float32,
        )
        * scale
    )
    scores = jnp.where(same[None, None], scores, jnp.float32(-1e30))
    weights = jax.nn.softmax(scores, axis=-1).astype(jnp.bfloat16)
    context = jnp.einsum(
        "phfg,gphd->fphd", weights, t_value.reshape(shape), preferred_element_type=jnp.float32
    )
    return context.astype(jnp.bfloat16).reshape(frames, part, width)


def shards(
    tokens,
    spatial_query,
    spatial_key,
    spatial_value,
    frame_counts,
    w_spatial_out,
    w_temporal_qkv,
    w_temporal_out,
):
    groups, frames_dev, patches, width = tokens.shape
    rows = frames_dev * patches
    head_size = width // HEADS
    out_cols, qkv_cols, final_cols = (
        lax.all_gather(w_spatial_out, "batch", axis=1, tiled=True),
        lax.all_gather(w_temporal_qkv, "batch", axis=1, tiled=True),
        lax.all_gather(w_temporal_out, "batch", axis=1, tiled=True),
    )
    shape = (frames_dev, patches, HEADS, head_size)
    scale = 1.0 / jnp.sqrt(jnp.float32(head_size))
    scores = (
        jnp.einsum(
            "fphd,fqhd->fhpq",
            spatial_query.reshape(shape),
            spatial_key.reshape(shape),
            preferred_element_type=jnp.float32,
        )
        * scale
    )
    weights = jax.nn.softmax(scores, axis=-1).astype(jnp.bfloat16)
    context = jnp.einsum(
        "fhpq,fqhd->fphd", weights, spatial_value.reshape(shape), preferred_element_type=jnp.float32
    )
    context = context.astype(jnp.bfloat16).reshape(rows, width)
    projected = fold_rows(context, lax.all_gather(out_cols, "seq", axis=0, tiled=True))
    hidden = (tokens.reshape(rows, width).astype(jnp.float32) + projected).astype(jnp.bfloat16)
    normed = layer_norm(hidden)
    count = lax.axis_size("seq")
    all_frames = frames_dev * count
    part = patches // count
    ends = jnp.cumsum(frame_counts[0])
    index = jnp.arange(all_frames, dtype=jnp.int32)
    clip = jnp.sum((index[:, None] >= ends[None, :]).astype(jnp.int32), axis=1)
    same = clip[:, None] == clip[None, :]
    qkv = fold_rows(normed, lax.all_gather(qkv_cols, "seq", axis=0, tiled=True))
    local = (1, frames_dev, patches, width)
    t_query = qkv[:, :width].astype(jnp.bfloat16).reshape(local)
    t_key = qkv[:, width : 2 * width].astype(jnp.bfloat16).reshape(local)
    t_value = qkv[:, 2 * width :].astype(jnp.bfloat16).reshape(local)
    t_query, t_key, t_value = (
        lax.all_to_all(t_query, "seq", split_axis=2, concat_axis=1, tiled=True),
        lax.all_to_all(t_key, "seq", split_axis=2, concat_axis=1, tiled=True),
        lax.all_to_all(t_value, "seq", split_axis=2, concat_axis=1, tiled=True),
    )
    temporal = temporal_attention(t_query[0], t_key[0], t_value[0], same)
    back = lax.all_to_all(
        temporal.reshape(1, all_frames, part, width), "seq", split_axis=1, concat_axis=2, tiled=True
    )
    back = back.reshape(rows, width)
    final = fold_rows(back, lax.all_gather(final_cols, "seq", axis=0, tiled=True))
    result = hidden.astype(jnp.float32) + final
    return result.astype(jnp.bfloat16).reshape(groups, frames_dev, patches, width)


def solution(mesh):
    placed = (
        P("batch", "seq", None, None),
        P("batch", "seq", None, None),
        P("batch", "seq", None, None),
        P("batch", "seq", None, None),
        P("batch", None),
        P("seq", "batch"),
        P("seq", "batch"),
        P("seq", "batch"),
    )
    return jax.shard_map(
        shards, mesh=mesh, in_specs=placed, out_specs=P("batch", "seq", None, None), check_vma=False
    )
```

profile of v0, /device:TPU:1, one launch (start us, length us, event | category | flops | bytes accessed | tf_op | source)
XLA Modules:
  0.0 535.1 jit_solution(11537488528974578990)
XLA Ops:
  6.5 10.6 %all-gather = bf16[4,288,9]{1,2,0:T(8,128)(2,1)S(1)} all-gather(bf16[1,288,9]{1,2,0:T(8,128)(2,1)} %bitcast.111), channel_id=1, replica_groups=mesh['seq'=128,'batch'=4] {'batch'}, dimensions={0}, use_global_device_ids=true | all-gather | bytes 25920 | tf_op jit(solution)/shard_map/all_gather | solution.py:58
  17.1 0.7 reshape.186
  17.8 0.0 all-gather.10.cloned.1.call-update
  17.9 0.0 all-gather.12.cloned.1.call-start
  17.9 9.3 %all-gather.2 = bf16[4,864,9]{1,2,0:T(8,128)(2,1)S(1)} all-gather(bf16[1,864,9]{1,2,0:T(8,128)(2,1)} %bitcast.110), channel_id=1, replica_groups=mesh['seq'=128,'batch'=4] {'batch'}, dimensions={0}, use_global_device_ids=true | all-gather | bytes 77760 | tf_op jit(solution)/shard_map/all_gather | solution.py:59
  27.2 0.8 reshape.190
  28.0 0.0 all-gather.12.cloned.1.call-update
  28.0 1.2 copy.62
  29.2 1.2 copy.63
  30.4 1.2 copy.64
  31.6 0.5 fusion.20
  32.1 0.4 convolution_multiply_fusion.1
  32.5 1.1 convolution_convert_fusion.2
  33.6 134.3 %all-gather.10.cloned.1.call-done = bf16[128,9,1152]{2,1,0:T(8,128)(2,1)} async-done(((bf16[1,9,1152]{2,1,0:T(8,128)(2,1)}), bf16[128,9,1152]{2,1,0:T(8,128)(2,1)}) %all-gather.10.cloned.1.call-update) | async-done | bytes 2654224 | tf_op jit(solution)/shard_map/all_gather | solution.py:78
  167.9 4.3 reshape.188
  172.3 1.7 fusion.21
  174.0 0.2 multiply_reduce_fusion
  174.2 147.1 %all-gather.12.cloned.1.call-done = bf16[128,9,3456]{2,1,0:T(8,128)(2,1)} async-done(((bf16[1,9,3456]{2,1,0:T(8,128)(2,1)}), bf16[128,9,3456]{2,1,0:T(8,128)(2,1)}) %all-gather.12.cloned.1.call-update) | async-done | bytes 7962640 | tf_op jit(solution)/shard_map/all_gather | solution.py:88
  321.3 14.4 %reshape.192 = bf16[1152,3456]{1,0:T(8,128)(2,1)} reshape(bf16[128,9,3456]{2,1,0:T(8,128)(2,1)} %all-gather.12.cloned.1.call-done) | data formatting | bytes 15925248
  335.7 4.7 convolution_convert_fusion
  340.3 0.0 copy-start.1
  340.4 0.1 slice_bitcast_fusion
  340.4 0.5 copy.89
  340.9 0.5 broadcast.75
  341.4 2.3 reduce.10
  343.8 1.1 reshape.200
  344.8 9.7 %all-to-all-start.1 = ((bf16[128,2,576]{2,1,0:T(2,128)(2,1)}), bf16[128,2,576]{2,1,0:T(2,128)(2,1)S(1)}, u32[]{:S(2)}, u32[]{:S(2)}) async-start(bf16[128,2,576]{2,1,0:T(2,128)(2,1)} %reshape.200), calls=%async_computation.1 | async-start | bytes 655360 | tf_op jit(solution)/shard_map/all_to_all | solution.py:94
  354.5 0.0 all-gather.14.cloned.1.call-start
  354.6 10.4 %all-gather.4 = bf16[4,288,9]{1,2,0:T(8,128)(2,1)S(1)} all-gather(bf16[1,288,9]{1,2,0:T(8,128)(2,1)S(1)} %bitcast.112), channel_id=1, replica_groups=mesh['seq'=128,'batch'=4] {'batch'}, dimensions={0}, use_global_device_ids=true | all-gather | bytes 25920 | tf_op jit(solution)/shard_map/all_gather | solution.py:60
  365.0 0.7 reshape.194
  365.7 0.0 all-gather.14.cloned.1.call-update
  365.7 0.5 copy.88
  366.2 0.0 copy-start.2
  366.2 2.3 reduce.11
  368.5 1.1 reshape.202
  369.6 8.0 %all-to-all-done.1 = bf16[128,2,576]{2,1,0:T(2,128)(2,1)S(1)} async-done(((bf16[128,2,576]{2,1,0:T(2,128)(2,1)}), bf16[128,2,576]{2,1,0:T(2,128)(2,1)S(1)}, u32[]{:S(2)}, u32[]{:S(2)}) %all-to-all-start.1) | async-done | bytes 294944 | tf_op jit(solution)/shard_map/all_to_all | solution.py:94
  377.5 10.2 %all-to-all-start.2 = ((bf16[128,2,576]{2,1,0:T(2,128)(2,1)}), bf16[128,2,576]{2,1,0:T(2,128)(2,1)S(1)}, u32[]{:S(2)}, u32[]{:S(2)}) async-start(bf16[128,2,576]{2,1,0:T(2,128)(2,1)} %reshape.202), calls=%async_computation.2 | async-start | bytes 655360 | tf_op jit(solution)/shard_map/all_to_all | solution.py:95
  387.8 0.5 copy.90
  388.2 2.3 reduce.9
  390.6 1.1 reshape.198
  391.6 19.6 %all-to-all-done.2 = bf16[128,2,576]{2,1,0:T(2,128)(2,1)S(1)} async-done(((bf16[128,2,576]{2,1,0:T(2,128)(2,1)}), bf16[128,2,576]{2,1,0:T(2,128)(2,1)S(1)}, u32[]{:S(2)}, u32[]{:S(2)}) %all-to-all-start.2) | async-done | bytes 294944 | tf_op jit(solution)/shard_map/all_to_all | solution.py:95
  411.2 9.1 %all-to-all-start = ((bf16[128,2,576]{2,1,0:T(2,128)(2,1)}), bf16[128,2,576]{2,1,0:T(2,128)(2,1)S(1)}, u32[]{:S(2)}, u32[]{:S(2)}) async-start(bf16[128,2,576]{2,1,0:T(2,128)(2,1)} %reshape.198), calls=%async_computation | async-start | bytes 655360 | tf_op jit(solution)/shard_map/all_to_all | solution.py:96
  420.3 0.1 copy.70
  420.4 0.1 reduce.8
  420.6 0.1 convert_reduce_fusion
  420.6 0.1 broadcast_compare_fusion
  420.7 0.5 reshape.201
  421.3 0.7 copy.72
  421.9 0.5 reshape.203
  422.5 0.7 copy.74
  423.2 21.1 %all-to-all-done = bf16[128,2,576]{2,1,0:T(2,128)(2,1)S(1)} async-done(((bf16[128,2,576]{2,1,0:T(2,128)(2,1)}), bf16[128,2,576]{2,1,0:T(2,128)(2,1)S(1)}, u32[]{:S(2)}, u32[]{:S(2)}) %all-to-all-start) | async-done | bytes 294944 | tf_op jit(solution)/shard_map/all_to_all | solution.py:96
  444.3 0.5 reshape.199
  444.8 0.7 copy.69
  445.5 0.5 fusion.22
  446.0 0.4 fusion.10
  446.4 0.4 convolution_convert_fusion.1
  446.8 0.8 copy.76
  447.5 2.3 reduce.12
  449.9 1.1 reshape.204
  450.9 8.7 %all-to-all-start.3 = ((bf16[128,2,576]{2,1,0:T(2,128)(2,1)}), bf16[128,2,576]{2,1,0:T(2,128)(2,1)}, u32[]{:S(2)}, u32[]{:S(2)}) async-start(bf16[128,2,576]{2,1,0:T(2,128)(2,1)} %reshape.204), calls=%async_computation.3 | async-start | bytes 655360 | tf_op jit(solution)/shard_map/all_to_all | solution.py:99
  459.6 59.0 %all-gather.14.cloned.1.call-done = bf16[128,9,1152]{2,1,0:T(8,128)(2,1)} async-done(((bf16[1,9,1152]{2,1,0:T(8,128)(2,1)}), bf16[128,9,1152]{2,1,0:T(8,128)(2,1)}) %all-gather.14.cloned.1.call-update) | async-done | bytes 2654224 | tf_op jit(solution)/shard_map/all_gather | solution.py:103
  518.6 4.3 reshape.196
  522.9 3.2 reshape.205
  526.2 2.4 fusion.5
  (12 shorter events, 0.1 us)
Async XLA Ops:
  6.5 161.4 %all-gather.10.cloned.1.call-start = ((), (), s32[]{:S(2)}) async-start(), calls=%async_computation.4 | async-start | bytes 4755456 | tf_op jit(solution)/shard_map/all_gather | solution.py:78
  17.9 303.4 %all-gather.12.cloned.1.call-start = ((), (), s32[]{:S(2)}) async-start(), calls=%async_computation.5 | async-start | bytes 14266368 | tf_op jit(solution)/shard_map/all_gather | solution.py:88
  33.6 138.7 %copy-start = (bf16[1,1,128,1152]{3,2,1,0:T(8,128)(2,1)S(1)}, bf16[1,1,128,1152]{3,2,1,0:T(8,128)(2,1)}, u32[]{:S(2)}) copy-start(bf16[1,1,128,1152]{3,2,1,0:T(8,128)(2,1)} %param.8) | copy-start | bytes 884740
  340.3 14.2 %copy-start.1 = (bf16[9,288]{1,0:T(8,128)(2,1)S(1)}, bf16[9,288]{1,0:T(8,128)(2,1)}, u32[]{:S(2)}) copy-start(bf16[9,288]{1,0:T(8,128)(2,1)} %param.15) | copy-start | bytes 15556
  344.8 32.7 %all-to-all-start.1 = ((bf16[128,2,576]{2,1,0:T(2,128)(2,1)}), bf16[128,2,576]{2,1,0:T(2,128)(2,1)S(1)}, u32[]{:S(2)}, u32[]{:S(2)}) async-start(bf16[128,2,576]{2,1,0:T(2,128)(2,1)} %reshape.200), calls=%async_computation.1 | async-start | bytes 655360 | tf_op jit(solution)/shard_map/all_to_all | solution.py:94
  354.5 164.0 %all-gather.14.cloned.1.call-start = ((), (), s32[]{:S(2)}) async-start(), calls=%async_computation.6 | async-start | bytes 4755456 | tf_op jit(solution)/shard_map/all_gather | solution.py:103
  366.2 54.1 %copy-start.2 = (s32[1,16]{1,0:T(1,128)S(1)}, s32[1,16]{1,0:T(1,128)}, u32[]{:S(2)}) copy-start(s32[1,16]{1,0:T(1,128)} %param.12) | copy-start | bytes 196
  377.5 33.7 %all-to-all-start.2 = ((bf16[128,2,576]{2,1,0:T(2,128)(2,1)}), bf16[128,2,576]{2,1,0:T(2,128)(2,1)S(1)}, u32[]{:S(2)}, u32[]{:S(2)}) async-start(bf16[128,2,576]{2,1,0:T(2,128)(2,1)} %reshape.202), calls=%async_computation.2 | async-start | bytes 655360 | tf_op jit(solution)/shard_map/all_to_all | solution.py:95
  411.2 33.1 %all-to-all-start = ((bf16[128,2,576]{2,1,0:T(2,128)(2,1)}), bf16[128,2,576]{2,1,0:T(2,128)(2,1)S(1)}, u32[]{:S(2)}, u32[]{:S(2)}) async-start(bf16[128,2,576]{2,1,0:T(2,128)(2,1)} %reshape.198), calls=%async_computation | async-start | bytes 655360 | tf_op jit(solution)/shard_map/all_to_all | solution.py:96
  450.9 72.0 %all-to-all-start.3 = ((bf16[128,2,576]{2,1,0:T(2,128)(2,1)}), bf16[128,2,576]{2,1,0:T(2,128)(2,1)}, u32[]{:S(2)}, u32[]{:S(2)}) async-start(bf16[128,2,576]{2,1,0:T(2,128)(2,1)} %reshape.204), calls=%async_computation.3 | async-start | bytes 655360 | tf_op jit(solution)/shard_map/all_to_all | solution.py:99
Sparse Core Ops, SparseCore 0:
  18.0 149.9 all-gather.9
  171.0 150.2 all-gather.11
  365.8 152.7 all-gather.13
where the time goes:
time: 536 us; the launch traced here: 535 us
  waiting for transfers between devices  389 us (73%)
  local copies, waits for them, and re-layouts  42.7 us (8%)
  starting transfers between devices  37.8 us (7%)
  blocking collectives  30.2 us (6%)
  between operations  13.4 us (2%)
  matrix products  12 us (2%)
  other arithmetic  9.85 us (2%)
    all_gather x1, waiting for transfers between devices, shards(): qkv = fold_rows(normed, lax.all_gather(qkv_cols, 'seq', axis=0, tiled=True))  147 us
    all_gather x1, waiting for transfers between devices, shards(): lax.all_gather(out_cols, 'seq', axis=0, tiled=True)  134 us
    all_gather x1, waiting for transfers between devices, shards(): lax.all_gather(final_cols, 'seq', axis=0, tiled=True)  59 us
    unnamed x24, local copies, waits for them, and re-layouts  38.3 us
    all_to_all x1, waiting for transfers between devices, shards(): lax.all_to_all(t_value, 'seq', split_axis=2, concat_axis=1, tiled=True)  21.1 us
    all_to_all x1, waiting for transfers between devices, shards(): lax.all_to_all(t_key, 'seq', split_axis=2, concat_axis=1, tiled=True)  19.6 us
  transfers between devices with their start and end apart: 7, of which 6 were waited for; matrix products, arithmetic and copies ran while one was open for 6% of the time, Pallas kernels for 0%

commit v1 on v0

v1 whole, which is shorter than its diff:
```python
import jax
import jax.numpy as jnp
from jax import lax
from jax.experimental import pallas as pl
from jax.experimental.pallas import tpu as pltpu
from jax.sharding import PartitionSpec as P

HEADS = 16
EPS = 1e-06
MESH = pl.DeviceIdType.MESH
BF16 = jnp.bfloat16
F32 = jnp.float32

ROWS = 128
WIDTH = 1152
SIZE = WIDTH // HEADS
LANES = 128
RAW = 1792
STEPS = 3
PAIR = 144


def dot(left, right):
    return jnp.dot(left, right, preferred_element_type=F32)


def iota(shape, dim):
    return lax.broadcasted_iota(jnp.int32, shape, dim)


def layer_norm(wide):
    mean = jnp.mean(wide, axis=1, keepdims=True)
    var = jnp.mean((wide - mean) ** 2, axis=1, keepdims=True)
    return ((wide - mean) * lax.rsqrt(var + EPS)).astype(BF16)


def attention(q_ref, k_ref, v_ref, same):
    scale = SIZE**-0.5
    parts = [[] for _ in range(WIDTH // LANES)]
    for head in range(HEADS):
        low = SIZE * head
        start = low // LANES * LANES
        span = LANES if low + SIZE <= start + LANES else 2 * LANES
        window = slice(start, start + span)
        lane = iota((1, span), 1) + start
        own = jnp.where((lane >= low) & (lane < low + SIZE), 1.0, 0.0).astype(BF16)
        scores = lax.dot_general(
            q_ref[:, window] * own, k_ref[:, window], (((1,), (1,)), ((), ())), preferred_element_type=F32
        )
        scores = scores * scale
        if same is not None:
            scores = jnp.where(same, scores, -1e30)
        top = jnp.max(scores, axis=1, keepdims=True)
        raised = jnp.exp(scores - top)
        weights = (raised * (1.0 / jnp.sum(raised, axis=1, keepdims=True))).astype(BF16)
        context = dot(weights, v_ref[:, window])
        for tile in range(span // LANES):
            parts[start // LANES + tile].append(
                (low + SIZE, context[:, tile * LANES : (tile + 1) * LANES])
            )
    lane = iota((ROWS, LANES), 1)
    tiles = []
    for index, found in enumerate(parts):
        total = found[-1][1]
        for end, value in reversed(found[:-1]):
            total = jnp.where(lane + index * LANES < end, value, total)
        tiles.append(total)
    return tiles


def kernel(
    counts, tok, sq, sk, sv, wraw, out,
    raw, piece, gat, wts, tokp, ctx, ctxp, zt, zc, xst, xsc, xrt, xrc,
    hid_f, hid_p, normed, qkv, tctx, rback, plane, zback,
    y_s, y_r, g_s, g_r, p_s, p_r, w_s, w_r, z_s, z_r, x_s, x_r,
):
    me = lax.axis_index("seq")
    y = lax.axis_index("batch")
    z = lax.div(me, 8)
    xc = lax.rem(me, 8)
    x = lax.div(xc, 2)
    c = lax.rem(me, 2)
    zp = lax.div(z, 2)
    zpar = lax.rem(z, 2)
    zmate = z + 1 - 2 * zpar
    cstar = lax.div(z, 8)
    active = c == cstar

    def at(z2, xc2, y2):
        return {"seq": z2 * 8 + xc2, "batch": y2}

    def ring(value, step, size):
        return lax.rem(value + (step + size), size)

    def remote(src, dst, send, recv, device):
        return pltpu.make_async_remote_copy(
            src_ref=src, dst_ref=dst, send_sem=send, recv_sem=recv, device_id=device, device_id_type=MESH
        )

    sends = []

    def send(src, dst, ss, rs, device):
        copy = remote(src, dst, ss, rs, device)
        copy.start()
        sends.append(copy)

    def arrived(dst, ss, rs):
        remote(dst, dst, ss, rs, at(z, xc, y)).wait_recv()

    barrier = pltpu.get_barrier_semaphore()
    peers = [at(z, xc, ring(y, d, 4)) for d in (1, 2, 3)]
    peers += [at(z, ring(xc, d, 8), y) for d in range(1, 8)]
    peers += [at(zmate, ring(xc, d, 8), y) for d in range(1, 8)]
    peers += [at(ring(z, d, 16), xc, y) for d in range(1, 16)]
    for peer in peers:
        pl.semaphore_signal(barrier, inc=1, device_id=peer, device_id_type=MESH)

    raw[y] = wraw[...]
    wide = tok[...].astype(F32)
    for i in range(16):
        tokp[i] = wide[8 * i : 8 * i + 8].astype(BF16)
    for i, tile in enumerate(attention(sq, sk, sv, None)):
        ctx[:, i * LANES : (i + 1) * LANES] = tile.astype(BF16)
        for r in range(16):
            ctxp[r, :, i * LANES : (i + 1) * LANES] = tile[8 * r : 8 * r + 8].astype(BF16)

    pl.semaphore_wait(barrier, len(peers))

    for d in (1, 2, 3):
        send(raw.at[y], raw.at[y], y_s.at[d], y_r.at[y], at(z, xc, ring(y, d, 4)))

    def z_exchange(n, src, dst):
        for d in range(1, 16):
            to = ring(z, d, 16)
            send(src.at[to], dst.at[z], z_s.at[n, d], z_r.at[n, z], at(to, xc, y))
        dst[z] = src[z]

    def z_wait(n, dst):
        for d in range(1, 16):
            source = ring(z, d, 16)
            arrived(dst.at[source], z_s.at[n, d], z_r.at[n, source])

    def x_exchange(n, src, dst):
        for d in range(1, 8):
            to = ring(xc, d, 8)
            send(src.at[to], dst.at[xc], x_s.at[n, d], x_r.at[n, xc], at(z, to, y))
        dst[xc] = src[xc]

    def x_wait(n, dst):
        for d in range(1, 8):
            source = ring(xc, d, 8)
            arrived(dst.at[source], x_s.at[n, d], x_r.at[n, source])

    def rows_of(ref):
        return jnp.concatenate([ref[i].astype(F32) for i in range(16)], axis=0).astype(BF16)

    def swap_rows(left, inner):
        outer = ROWS // inner
        i, k = iota((ROWS, ROWS), 0), iota((ROWS, ROWS), 1)
        pick = k == lax.rem(i, inner) * outer + lax.div(i, inner)
        return dot(jnp.where(pick, 1.0, 0.0).astype(BF16), left)

    z_exchange(0, tokp, zt)

    for d in (1, 2, 3):
        source = ring(y, d, 4)
        arrived(raw.at[source], y_s.at[d], y_r.at[source])

    row, col = iota((3 * LANES, LANES), 0), iota((3 * LANES, LANES), 1)
    for j in range(STEPS):
        for x2 in range(4):
            tile = jnp.minimum(16 * j + 4 * x2 + y, 44)
            second = jnp.where(tile >= 9, 1, 0)
            third = jnp.where(tile >= 36, 1, 0)
            block = 288 + 576 * (second - third)
            lanes = 384 * second + 896 * third
            begin = LANES * (tile - 9 * second - 27 * third)
            y1 = jnp.where(second - third == 1, lax.div(begin, 864), lax.div(begin, 288))
            y2 = jnp.minimum(y1 + 1, 3)
            inside = begin - y1 * block
            skip = lax.rem(inside, LANES)
            first = jnp.minimum(block - inside, LANES)
            near = (row == col + skip) & (col < first)
            far = (row == col - first + 2 * LANES) & (col >= first)
            pick = jnp.where(near | far, 1.0, 0.0).astype(BF16)
            start = pl.multiple_of(lanes + inside - skip, LANES)
            left = raw[y1, :, pl.ds(start, 2 * LANES)]
            right = raw[y2, :, pl.ds(pl.multiple_of(lanes, LANES), LANES)]
            piece[x2, j] = dot(jnp.concatenate([left, right], axis=1), pick).astype(BF16)

    source = 8 * zpar + xc
    for zo in (0, 1):
        for dx in range(4):
            x2 = ring(x, dx, 4)
            where = at(z if zo == 0 else zmate, 2 * x2 + cstar, y)
            sem = g_s.at[4 * zo + dx]
            if zo == 0 and dx == 0:

                @pl.when(active)
                def _():
                    gat[source] = piece[x]

                @pl.when(jnp.logical_not(active))
                def _():
                    remote(piece.at[x2], gat.at[source], sem, g_r.at[source], where).start()
            else:
                send(piece.at[x2], gat.at[source], sem, g_r.at[source], where)

    @pl.when(active)
    def _():
        for d in range(1, 16):
            other = ring(source, d, 16)
            arrived(gat.at[other], g_s.at[0], g_r.at[other])
        i, k = iota((PAIR, 256), 0), iota((PAIR, 256), 1)
        pick = jnp.where(k == 16 * lax.div(i, 9) + lax.rem(i, 9), 1.0, 0.0).astype(BF16)
        for j in range(STEPS):
            wts[j, x, y, zp] = dot(pick, gat[:, j].reshape(256, LANES)).astype(BF16)
            for d in range(1, 8):
                to = ring(z, d * (2 * zpar - 1), 16)
                spot = wts.at[j, x, y, zp]
                remote(spot, spot, p_s.at[j, d], p_r.at[j, zp], at(to, xc, y)).start()

    z_exchange(1, ctxp, zc)

    up, down = (lambda v: ring(v, 1, 4)), (lambda v: ring(v, -1, 4))
    far = lambda v: ring(v, 2, 4)

    def chain(j, order):
        base = 4 * c + 2 * order
        both, low, high = pl.ds(base, 2), pl.ds(base, 1), pl.ds(base + 1, 1)
        u, v = (x, y) if order == 0 else (y, x)

        def ref(uu, vv, part):
            if order == 0:
                return wts.at[j, uu, vv, part]
            return wts.at[j, vv, uu, part]

        def line(vv, part):
            if order == 0:
                return wts.at[j, :, vv, part]
            return wts.at[j, vv, :, part]

        def device(uu, vv):
            return at(z, 2 * uu + c, vv) if order == 0 else at(z, 2 * vv + c, uu)

        def go(n, spot, uu, vv):
            send(spot, spot, w_s.at[j, order, n], w_r.at[j, order, n], device(uu, vv))

        def got(n, spot):
            arrived(spot, w_s.at[j, order, n], w_r.at[j, order, n])

        def share(n, spot):
            send(spot, spot, w_s.at[j, order, n], w_r.at[j, order, n], at(z, 2 * x + 1 - c, y))

        def shared(n, vv):
            spot = (
                wts.at[j, :, vv, pl.ds(4 * (1 - c) + 2 * order, 2)]
                if order == 0
                else wts.at[j, vv, :, pl.ds(4 * (1 - c) + 2 * order, 2)]
            )
            arrived(spot, w_s.at[j, order, n], w_r.at[j, order, n])

        def s0():
            go(0, ref(u, v, both), up(u), v)
            go(1, ref(u, v, both), down(u), v)
            go(4, ref(u, v, both), u, up(v))
            go(5, ref(u, v, both), u, down(v))

        def s1():
            got(0, ref(down(u), v, both))
            go(2, ref(down(u), v, low), up(u), v)
            go(6, ref(down(u), v, both), u, up(v))
            go(7, ref(down(u), v, both), u, down(v))
            got(1, ref(up(u), v, both))
            go(3, ref(up(u), v, high), down(u), v)
            go(8, ref(up(u), v, both), u, up(v))
            go(9, ref(up(u), v, both), u, down(v))

        def s2():
            got(2, ref(far(u), v, low))
            got(3, ref(far(u), v, high))
            go(10, ref(far(u), v, both), u, up(v))
            go(11, ref(far(u), v, both), u, down(v))
            share(14, line(v, both))

        def s3():
            for k, uu in enumerate((u, down(u), up(u), far(u))):
                got(4 + 2 * k, ref(uu, down(v), both))
            go(12, line(down(v), low), u, up(v))
            share(15, line(down(v), both))
            for k, uu in enumerate((u, down(u), up(u), far(u))):
                got(5 + 2 * k, ref(uu, up(v), both))
            go(13, line(up(v), high), u, down(v))
            share(16, line(up(v), both))

        def s4():
            got(12, line(far(v), low))
            got(13, line(far(v), high))
            share(17, line(far(v), both))

        def s5():
            shared(14, v)
            shared(15, down(v))
            shared(16, up(v))
            shared(17, far(v))

        return s0, s1, s2, s3, s4, s5

    chains = [[chain(j, 0), chain(j, 1)] for j in range(STEPS)]

    def stage(j, s):
        if s == 0:
            for k in range(4):

                @pl.when(4 * c + k != zp)
                def _():
                    arrived(wts.at[j, x, y, 4 * c + k], p_s.at[j, 1], p_r.at[j, 4 * c + k])
        chains[j][0][s]()
        chains[j][1][s]()

    def tiles(left, first, count, emit):
        def body(n, carry):
            right = []
            for i in range(3):
                t = first + 3 * n + i
                k = lax.rem(t, 16)
                right.append(wts[lax.div(t, 16), lax.div(k, 4), lax.rem(k, 4)].reshape(WIDTH, LANES))
            emit(n, dot(left[...], jnp.concatenate(right, axis=1)))
            return carry

        lax.fori_loop(0, count, body, 0)

    def columns(n):
        return pl.ds(pl.multiple_of(n * 384, LANES), 384)

    stage(0, 0)
    stage(0, 1)
    stage(0, 2)
    stage(1, 0)

    z_wait(0, zt)
    moved = swap_rows(rows_of(zt), 16)
    for i in range(8):
        xst[i] = moved[16 * i : 16 * i + 16].astype(BF16)
    x_exchange(0, xst, xrt)

    stage(0, 3)
    stage(1, 1)
    stage(2, 0)

    z_wait(1, zc)
    moved = swap_rows(rows_of(zc), 16)
    for i in range(8):
        xsc[i] = moved[16 * i : 16 * i + 16].astype(BF16)
    x_exchange(1, xsc, xrc)

    stage(0, 4)
    stage(1, 2)
    stage(2, 1)
    stage(0, 5)
    stage(1, 3)
    stage(2, 2)

    def clip_of(dim):
        place = iota((ROWS, ROWS), dim)
        frame = lax.rem(place, 16) * 8 + lax.div(place, 16)
        end = jnp.int32(0)
        clip = jnp.zeros((ROWS, ROWS), jnp.int32)
        for n in range(16):
            end = end + counts[0, n]
            clip = clip + jnp.where(frame >= end, 1, 0)
        return clip

    same = clip_of(0) == clip_of(1)

    x_wait(0, xrt)
    x_wait(1, xrc)

    def hidden_here(n, product):
        hid_f[:, columns(n)] = (tok[:, columns(n)].astype(F32) + product).astype(BF16)

    def hidden_there(n, product):
        base = xrt[:, :, columns(n)].reshape(ROWS, 384).astype(F32)
        hid_p[:, columns(n)] = (base + product).astype(BF16)

    rback[...] = xrc[...].reshape(ROWS, WIDTH)
    tiles(rback, 0, 3, hidden_there)
    normed[...] = layer_norm(hid_p[...].astype(F32))
    tiles(ctx, 0, 3, hidden_here)

    stage(1, 4)
    stage(2, 3)
    stage(1, 5)

    def keep(n, product):
        qkv[lax.div(n, 3), :, columns(lax.rem(n, 3))] = product.astype(BF16)

    tiles(normed, 9, 7, keep)
    stage(2, 4)
    stage(2, 5)
    tiles(normed, 30, 2, lambda n, product: keep(n + 7, product))

    for i, tile in enumerate(attention(qkv.at[0], qkv.at[1], qkv.at[2], same)):
        for r in range(8):
            tctx[r, :, i * LANES : (i + 1) * LANES] = tile[16 * r : 16 * r + 16].astype(BF16)

    x_exchange(2, tctx, plane)
    x_wait(2, plane)
    moved = swap_rows(plane[...].reshape(ROWS, WIDTH), 8)
    for i in range(16):
        zback[0, i] = moved[8 * i : 8 * i + 8].astype(BF16)
    z_exchange(2, zback.at[0], zback.at[1])
    z_wait(2, zback.at[1])
    rback[...] = rows_of(zback.at[1])

    def last(n, product):
        out[:, columns(n)] = (hid_f[:, columns(n)].astype(F32) + product).astype(BF16)

    tiles(rback, 36, 3, last)

    for copy in sends:
        copy.wait_send()

    @pl.when(active)
    def _():
        for j in range(STEPS):
            for d in range(1, 8):
                spot = wts.at[j, x, y, zp]
                remote(spot, spot, p_s.at[j, d], p_r.at[j, zp], at(z, xc, y)).wait_send()

    @pl.when(jnp.logical_not(active))
    def _():
        remote(piece.at[x], gat.at[source], g_s.at[0], g_r.at[source], at(z, xc, y)).wait_send()


def shards(
    tokens,
    spatial_query,
    spatial_key,
    spatial_value,
    frame_counts,
    w_spatial_out,
    w_temporal_qkv,
    w_temporal_out,
):
    def padded(array, lanes):
        return jnp.pad(array, ((0, 16 - array.shape[0]), (0, lanes - array.shape[1])))

    wraw = jnp.concatenate(
        [padded(w_spatial_out, 384), padded(w_temporal_qkv, 896), padded(w_temporal_out, 512)], axis=1
    )
    flat = (ROWS, WIDTH)
    vmem = pl.BlockSpec(memory_space=pltpu.VMEM)
    dma = pltpu.SemaphoreType.DMA
    result = pl.pallas_call(
        kernel,
        out_shape=jax.ShapeDtypeStruct(flat, BF16),
        in_specs=[pl.BlockSpec(memory_space=pltpu.SMEM)] + [vmem] * 5,
        out_specs=vmem,
        scratch_shapes=[
            pltpu.VMEM((4, 16, RAW), BF16),
            pltpu.VMEM((4, STEPS, 16, LANES), BF16),
            pltpu.VMEM((16, STEPS, 16, LANES), BF16),
            pltpu.VMEM((STEPS, 4, 4, 8, PAIR, LANES), BF16),
            pltpu.VMEM((16, 8, WIDTH), BF16),
            pltpu.VMEM(flat, BF16),
            pltpu.VMEM((16, 8, WIDTH), BF16),
            pltpu.VMEM((16, 8, WIDTH), BF16),
            pltpu.VMEM((16, 8, WIDTH), BF16),
            pltpu.VMEM((8, 16, WIDTH), BF16),
            pltpu.VMEM((8, 16, WIDTH), BF16),
            pltpu.VMEM((8, 16, WIDTH), BF16),
            pltpu.VMEM((8, 16, WIDTH), BF16),
            pltpu.VMEM(flat, BF16),
            pltpu.VMEM(flat, BF16),
            pltpu.VMEM(flat, BF16),
            pltpu.VMEM((3,) + flat, BF16),
            pltpu.VMEM((8, 16, WIDTH), BF16),
            pltpu.VMEM(flat, BF16),
            pltpu.VMEM((8, 16, WIDTH), BF16),
            pltpu.VMEM((2, 16, 8, WIDTH), BF16),
            dma((4,)), dma((4,)),
            dma((8,)), dma((16,)),
            dma((STEPS, 8)), dma((STEPS, 8)),
            dma((STEPS, 2, 18)), dma((STEPS, 2, 18)),
            dma((3, 16)), dma((3, 16)),
            dma((3, 8)), dma((3, 8)),
        ],
        compiler_params=pltpu.CompilerParams(
            collective_id=0, has_side_effects=True, vmem_limit_bytes=50 * 2**20
        ),
    )(
        frame_counts,
        tokens.reshape(flat),
        spatial_query.reshape(flat),
        spatial_key.reshape(flat),
        spatial_value.reshape(flat),
        wraw,
    )
    return result.reshape(tokens.shape)


def solution(mesh):
    placed = (
        P("batch", "seq", None, None),
        P("batch", "seq", None, None),
        P("batch", "seq", None, None),
        P("batch", "seq", None, None),
        P("batch", None),
        P("seq", "batch"),
        P("seq", "batch"),
        P("seq", "batch"),
    )
    return jax.shard_map(
        shards, mesh=mesh, in_specs=placed, out_specs=P("batch", "seq", None, None), check_vma=False
    )
```

time: 536 us -> 135 us (0.25)
  waiting for transfers between devices: 389 us -> 0 us
  Pallas kernels: 0 us -> 130 us
  local copies, waits for them, and re-layouts: 42.7 us -> 4.56 us
  starting transfers between devices: 37.8 us -> 0 us
  blocking collectives: 30.2 us -> 0 us
  between operations: 13.4 us -> 0.03 us
  matrix products: 12 us -> 0 us
  other arithmetic: 9.85 us -> 0.79 us
    all_gather x3 -> x0, waiting for transfers between devices: 340 us -> none  [the longest x1 147 us: shards(): qkv = fold_rows(normed, lax.all_gather(qkv_cols, 'seq', axis=0, tiled=True))]
    pallas_call x0 -> x1, Pallas kernels: none -> 130 us  [shards(): pl.pallas_call(kernel, out_shape=jax.ShapeDtypeStruct(flat, BF16), in_spe...]
    all_to_all x4 -> x0, waiting for transfers between devices: 48.7 us -> none  [the longest x1 21.1 us: shards(): lax.all_to_all(t_value, 'seq', split_axis=2, concat_axis=1, tiled=True)]
    all_to_all x4 -> x0, starting transfers between devices: 37.7 us -> none  [the longest x1 10.2 us: shards(): lax.all_to_all(t_key, 'seq', split_axis=2, concat_axis=1, tiled=True)]
    unnamed x24 -> x11, local copies, waits for them, and re-layouts: 38.3 us -> 4.56 us
    all_gather x3 -> x0, blocking collectives: 30.2 us -> none  [the longest x1 10.6 us: shards(): lax.all_gather(w_spatial_out, 'batch', axis=1, tiled=True)]
    dot_general x7 -> x0, matrix products: 11 us -> none  [the longest x3 8.72 us: fold_rows(): return jnp.dot(left, piece, preferred_element_type=jnp.float32)]
    unnamed x4 -> x0, other arithmetic: 9.3 us -> none
  transfers between devices with their start and end apart: 7 -> 0, of which waited for: 6 -> 0; matrix products, arithmetic and copies ran while one was open for 6% -> 0% of each run, Pallas kernels for 0% -> 0%
where the time goes in v1:
time: 135 us
  Pallas kernels  130 us (96%)
  local copies, waits for them, and re-layouts  4.56 us (3%)
    pallas_call x1, Pallas kernels, shards(): pl.pallas_call(kernel, out_shape=jax.ShapeDtypeStruct(flat, BF16), in_spe...  130 us
    unnamed x11, local copies, waits for them, and re-layouts  4.56 us

profile of v1, /device:TPU:1, one launch (start us, length us, event | category | flops | bytes accessed | tf_op | source)
XLA Modules:
  0.0 135.1 jit_solution(11608908560780516398)
XLA Ops:
  0.0 0.0 copy-start.4
  0.0 0.8 fusion.5.wraw
  0.8 0.0 copy-done.4
  0.8 0.0 copy-start
  0.8 1.0 copy-done
  1.8 0.0 copy-start.1
  1.8 1.0 copy-done.1
  2.7 0.0 copy-start.2
  2.7 1.0 copy-done.2
  3.7 0.0 copy-start.3
  3.7 1.0 copy-done.3
  4.7 129.7 %shard_map.82 = bf16[128,1152]{1,0:T(8,128)(2,1)S(1)} custom-call(s32[1,16]{1,0:T(1,128)S(1)} %copy-done.4, bf16[128,1152]{1,0:T(8,128)(2,1)S(1)} %bitcast.6, bf16[128,1152]{1,0:T(8,128)(2,1)S(1)} %bitcast.7, bf16[128,1152]{1,0:T(8,128)(2,1)S(1)} %bitcast.8, bf16[128,1152]{1,0:T(8,128)(2,1)S(1)} %bitcast.9, bf16[16,1792]{1,0:T(8,128)(2,1)S(1)} %fusion.5.wraw), custom_call_target="tpu_custom_call" | custom-call | tf_op jit(solution)/shard_map/pallas_call | solution.py:455
  134.4 0.7 copy.10
Async XLA Ops:
  0.0 0.8 copy-start.4
  0.8 1.0 copy-start
  1.8 1.0 copy-start.1
  2.7 1.0 copy-start.2
  3.7 1.0 copy-start.3

commit v2 on v1

v2 whole, which is shorter than its diff:
```python
import jax
import jax.numpy as jnp
from jax import lax
from jax.experimental import pallas as pl
from jax.experimental.pallas import tpu as pltpu
from jax.sharding import PartitionSpec as P

HEADS = 16
EPS = 1e-06
LOG2E = 1.4426950408889634
MESH = pl.DeviceIdType.MESH
BF16 = jnp.bfloat16
F32 = jnp.float32

ROWS = 128
WIDTH = 1152
SIZE = WIDTH // HEADS
LANES = 128
RAW = 1792
STEPS = 3
PAIR = 144
EARLY = 640

ORDER = list(range(9)) + [9, 10, 11, 18, 19, 20, 27]
ORDER += [28, 29, 12, 13, 14, 21, 22, 23, 30, 31, 32, 15, 16, 17, 24, 25]
ORDER += [26, 33, 34, 35] + list(range(36, 45)) + [44, 44, 44]


def dot(left, right):
    return jnp.dot(left, right, preferred_element_type=F32)


def iota(shape, dim):
    return lax.broadcasted_iota(jnp.int32, shape, dim)


def layer_norm(wide):
    mean = jnp.mean(wide, axis=1, keepdims=True)
    var = jnp.mean((wide - mean) ** 2, axis=1, keepdims=True)
    return ((wide - mean) * lax.rsqrt(var + EPS)).astype(BF16)


class Attention:
    def __init__(self, q_ref, k_ref, v_ref, same):
        self.q, self.k, self.v, self.same = q_ref, k_ref, v_ref, same
        self.parts = [[] for _ in range(WIDTH // LANES)]

    def heads(self, first, last):
        for head in range(first, last):
            low = SIZE * head
            start = low // LANES * LANES
            span = LANES if low + SIZE <= start + LANES else 2 * LANES
            window = slice(start, start + span)
            lane = iota((1, span), 1) + start
            own = jnp.where((lane >= low) & (lane < low + SIZE), 1.0, 0.0).astype(BF16)
            scores = lax.dot_general(
                self.q[:, window] * own, self.k[:, window], (((1,), (1,)), ((), ())), preferred_element_type=F32
            )
            if self.same is not None:
                scores = jnp.where(self.same, scores, -1e30)
            top = jnp.max(scores, axis=1, keepdims=True)
            raised = jnp.exp2((scores - top) * (SIZE**-0.5 * LOG2E))
            inverse = 1.0 / jnp.sum(raised, axis=1, keepdims=True)
            context = dot(raised.astype(BF16), self.v[:, window])
            for tile in range(span // LANES):
                value = context[:, tile * LANES : (tile + 1) * LANES] * inverse
                self.parts[start // LANES + tile].append((low + SIZE, value))

    def tile(self, index):
        lane = iota((ROWS, LANES), 1) + index * LANES
        found = self.parts[index]
        total = found[-1][1]
        for end, value in reversed(found[:-1]):
            total = jnp.where(lane < end, value, total)
        return total


def kernel(
    counts, tok_in, sq_in, sk_in, sv_in, wraw, out,
    tok, sq, sk, sv, raw, picks, piece, gat, wts, ctx, xt, xc_in, zst, zsc, zt, zc,
    hid_f, hid_p, normed, qkv, zs_a, zs_b, zr_a, zr_b, xs_a, xs_b, xr_a, xr_b, rback, total,
    in_s, y_s, y_r, g_s, g_r, p_s, p_r, w_s, w_r, z_s, z_r, x_s, x_r,
):
    me = lax.axis_index("seq")
    y = lax.axis_index("batch")
    z = lax.div(me, 8)
    xc = lax.rem(me, 8)
    x = lax.div(xc, 2)
    c = lax.rem(me, 2)
    zp = lax.div(z, 2)
    zpar = lax.rem(z, 2)
    zmate = z + 1 - 2 * zpar
    cstar = lax.div(z, 8)
    active = c == cstar

    def at(z2, xc2, y2):
        return {"seq": z2 * 8 + xc2, "batch": y2}

    def ring(value, step, size):
        return lax.rem(value + (step + size), size)

    def remote(src, dst, send, recv, device):
        return pltpu.make_async_remote_copy(
            src_ref=src, dst_ref=dst, send_sem=send, recv_sem=recv, device_id=device, device_id_type=MESH
        )

    sends = []
    maybe = []

    def send(src, dst, ss, rs, device):
        copy = remote(src, dst, ss, rs, device)
        copy.start()
        sends.append(copy)

    def send_if(on, src, dst, ss, rs, device):
        copy = remote(src, dst, ss, rs, device)
        pl.when(on)(copy.start)
        maybe.append((on, copy))

    def arrived(dst, ss, rs):
        remote(dst, dst, ss, rs, at(z, xc, y)).wait_recv()

    barrier = pltpu.get_barrier_semaphore()
    peers = [at(z, xc, ring(y, d, 4)) for d in (1, 2, 3)]
    peers += [at(z, ring(xc, d, 8), y) for d in range(1, 8)]
    peers += [at(zmate, ring(xc, d, 8), y) for d in range(1, 8)]
    peers += [at(ring(z, d, 16), xc, y) for d in range(1, 16)]
    for peer in peers:
        pl.semaphore_signal(barrier, inc=1, device_id=peer, device_id_type=MESH)

    loads = [
        pltpu.make_async_copy(src, dst, in_s.at[n])
        for n, (src, dst) in enumerate(
            ((wraw, raw.at[y]), (tok_in, tok), (sq_in, sq), (sk_in, sk), (sv_in, sv))
        )
    ]
    for load in loads:
        load.start()
    places = []
    row, col = iota((3 * LANES, LANES), 0), iota((3 * LANES, LANES), 1)
    for j in range(STEPS):
        for x2 in range(4):
            tile = sum(jnp.where(y == i, ORDER[16 * j + 4 * x2 + i], 0) for i in range(4))
            second = jnp.where(tile >= 9, 1, 0)
            third = jnp.where(tile >= 36, 1, 0)
            block = 288 + 576 * (second - third)
            lanes = 384 * second + 896 * third
            begin = LANES * (tile - 9 * second - 27 * third)
            y1 = jnp.where(second - third == 1, lax.div(begin, 864), lax.div(begin, 288))
            y2 = jnp.minimum(y1 + 1, 3)
            inside = begin - y1 * block
            skip = lax.rem(inside, LANES)
            first = jnp.minimum(block - inside, LANES)
            near = (row == col + skip) & (col < first)
            far = (row == col - first + 2 * LANES) & (col >= first)
            picks[j, x2] = jnp.where(near | far, 1.0, 0.0).astype(BF16)
            places.append((j, x2, y1, pl.multiple_of(lanes + inside - skip, LANES), y2, pl.multiple_of(lanes, LANES)))

    for load in loads[2:]:
        load.wait()
    spatial = Attention(sq, sk, sv, None)
    spatial.heads(0, HEADS)
    for i in range(9):
        ctx[:, i * LANES : (i + 1) * LANES] = spatial.tile(i).astype(BF16)
    loads[0].wait()
    loads[1].wait()

    pl.semaphore_wait(barrier, len(peers))

    for d in (1, 2, 3):
        send(raw.at[y], raw.at[y], y_s.at[d], y_r.at[y], at(z, xc, ring(y, d, 4)))

    def z_exchange(n, src, dst):
        for d in range(1, 16):
            to = ring(z, d, 16)
            send(src.at[to], dst.at[z], z_s.at[n, d], z_r.at[n, z], at(to, xc, y))
        dst[z] = src[z]

    def z_wait(n, dst):
        for d in range(1, 16):
            source = ring(z, d, 16)
            arrived(dst.at[source], z_s.at[n, d], z_r.at[n, source])

    def block(src, index):
        if len(src.shape) == 3:
            return src.at[index]
        return src.at[pl.ds(pl.multiple_of(index * 16, 16), 16)]

    def x_exchange(n, src, dst):
        for d in range(1, 8):
            to = ring(xc, d, 8)
            send(block(src, to), dst.at[xc], x_s.at[n, d], x_r.at[n, xc], at(z, to, y))
        dst[xc] = block(src, xc)[...]

    def x_wait(n, dst):
        for d in range(1, 8):
            source = ring(xc, d, 8)
            arrived(dst.at[source], x_s.at[n, d], x_r.at[n, source])

    def rows_of(ref):
        return jnp.concatenate([ref[i].astype(F32) for i in range(16)], axis=0).astype(BF16)

    def swap_rows(left, inner):
        outer = ROWS // inner
        i, k = iota((ROWS, ROWS), 0), iota((ROWS, ROWS), 1)
        pick = k == lax.rem(i, inner) * outer + lax.div(i, inner)
        return dot(jnp.where(pick, 1.0, 0.0).astype(BF16), left)

    x_exchange(0, ctx, xc_in)
    x_exchange(1, tok, xt)

    for d in (1, 2, 3):
        source = ring(y, d, 4)
        arrived(raw.at[source], y_s.at[d], y_r.at[source])

    for j, x2, y1, start1, y2, start2 in places:
        left = raw[y1, :, pl.ds(start1, 2 * LANES)]
        right = raw[y2, :, pl.ds(start2, LANES)]
        piece[x2, j] = dot(jnp.concatenate([left, right], axis=1), picks[j, x2]).astype(BF16)

    source = 8 * zpar + xc
    for zo in (0, 1):
        for dx in range(4):
            x2 = ring(x, dx, 4)
            where = at(z if zo == 0 else zmate, 2 * x2 + cstar, y)
            sem = g_s.at[4 * zo + dx]
            if zo == 0 and dx == 0:

                @pl.when(active)
                def _():
                    gat[source] = piece[x]

                send_if(jnp.logical_not(active), piece.at[x2], gat.at[source], sem, g_r.at[source], where)
            else:
                send(piece.at[x2], gat.at[source], sem, g_r.at[source], where)

    @pl.when(active)
    def _():
        for d in range(1, 16):
            other = ring(source, d, 16)
            arrived(gat.at[other], g_s.at[0], g_r.at[other])
        i, k = iota((PAIR, 256), 0), iota((PAIR, 256), 1)
        pick = jnp.where(k == 16 * lax.div(i, 9) + lax.rem(i, 9), 1.0, 0.0).astype(BF16)
        for j in range(STEPS):
            wts[j, x, y, zp] = dot(pick, gat[:, j].reshape(256, LANES)).astype(BF16)

    way = 2 * zpar - 1

    def passed(m):
        return ring(zp, -m * way, 8)

    def along(j, m, hops):
        block = passed(m)
        on = c == lax.div(block, 4)
        spot = wts.at[j, x, y, block]
        if m > 0:

            @pl.when(on)
            def _():
                arrived(spot, p_s.at[j, 0, 0], p_r.at[j, block])

        for hop in hops:
            to = ring(z, hop * way, 16)
            send_if(on, spot, spot, p_s.at[j, min(m, 1), hop - 1], p_r.at[j, block], at(to, xc, y))

    def to_z(n, landed, src, dst):
        x_wait(n, landed)
        moved = swap_rows(landed[...].reshape(ROWS, WIDTH), 8)
        for i in range(16):
            src[i] = moved[8 * i : 8 * i + 8].astype(BF16)
        z_exchange(n, src, dst)

    for j in range(STEPS):
        along(j, 0, (4, 3, 2, 1))
    to_z(0, xc_in, zsc, zc)
    along(0, 2, (3, 2, 1))
    to_z(1, xt, zst, zt)
    along(1, 2, (3, 2, 1))
    along(2, 2, (3, 2, 1))

    up, down = (lambda v: ring(v, 1, 4)), (lambda v: ring(v, -1, 4))
    far = lambda v: ring(v, 2, 4)

    def chain(j, order):
        base = 4 * c + 2 * order
        both, low, high = pl.ds(base, 2), pl.ds(base, 1), pl.ds(base + 1, 1)
        u, v = (x, y) if order == 0 else (y, x)

        def ref(uu, vv, part):
            if order == 0:
                return wts.at[j, uu, vv, part]
            return wts.at[j, vv, uu, part]

        def line(vv, part):
            if order == 0:
                return wts.at[j, :, vv, part]
            return wts.at[j, vv, :, part]

        def device(uu, vv):
            return at(z, 2 * uu + c, vv) if order == 0 else at(z, 2 * vv + c, uu)

        def go(n, spot, uu, vv):
            send(spot, spot, w_s.at[j, order, n], w_r.at[j, order, n], device(uu, vv))

        def got(n, spot):
            arrived(spot, w_s.at[j, order, n], w_r.at[j, order, n])

        def share(n, spot):
            send(spot, spot, w_s.at[j, order, n], w_r.at[j, order, n], at(z, 2 * x + 1 - c, y))

        def shared(n, vv):
            spot = (
                wts.at[j, :, vv, pl.ds(4 * (1 - c) + 2 * order, 2)]
                if order == 0
                else wts.at[j, vv, :, pl.ds(4 * (1 - c) + 2 * order, 2)]
            )
            arrived(spot, w_s.at[j, order, n], w_r.at[j, order, n])

        def s0():
            go(2, ref(u, v, both), far(u), v)
            go(0, ref(u, v, both), up(u), v)
            go(1, ref(u, v, both), down(u), v)
            go(4, ref(u, v, both), u, up(v))
            go(5, ref(u, v, both), u, down(v))

        def s1():
            got(0, ref(down(u), v, both))
            go(6, ref(down(u), v, both), u, up(v))
            go(7, ref(down(u), v, both), u, down(v))
            got(1, ref(up(u), v, both))
            go(8, ref(up(u), v, both), u, up(v))
            go(9, ref(up(u), v, both), u, down(v))
            got(2, ref(far(u), v, both))
            go(10, ref(far(u), v, both), u, up(v))
            go(11, ref(far(u), v, both), u, down(v))
            share(14, line(v, both))

        def s2():
            for k, uu in enumerate((u, down(u), up(u), far(u))):
                got(4 + 2 * k, ref(uu, down(v), both))
            go(12, line(down(v), low), u, up(v))
            share(15, line(down(v), both))
            for k, uu in enumerate((u, down(u), up(u), far(u))):
                got(5 + 2 * k, ref(uu, up(v), both))
            go(13, line(up(v), high), u, down(v))
            share(16, line(up(v), both))

        def s3():
            got(12, line(far(v), low))
            got(13, line(far(v), high))
            share(17, line(far(v), both))

        def s4():
            shared(14, v)
            shared(15, down(v))
            shared(16, up(v))
            shared(17, far(v))

        return s0, s1, s2, s3, s4

    chains = [[chain(j, 0), chain(j, 1)] for j in range(STEPS)]

    def stage(j, s):
        if s == 0:
            for m in (1, 3, 4, 5, 6, 7):
                block = passed(m)

                @pl.when(c == lax.div(block, 4))
                def _():
                    arrived(wts.at[j, x, y, block], p_s.at[j, 0, 0], p_r.at[j, block])

        chains[j][0][s]()
        chains[j][1][s]()

    def weights(first, count=3, depth=slice(0, WIDTH)):
        right = []
        for t in range(first, first + count):
            j, k = divmod(ORDER.index(t), 16)
            right.append(wts[j, k // 4, k % 4].reshape(WIDTH, LANES)[depth])
        return jnp.concatenate(right, axis=1)

    def columns(n):
        return slice(384 * n, 384 * n + 384)

    stage(0, 0)
    stage(1, 0)
    stage(0, 1)
    stage(2, 0)
    stage(1, 1)
    stage(0, 2)
    stage(2, 1)
    stage(0, 3)
    stage(1, 2)
    stage(0, 4)

    def clip_of(dim):
        frame = iota((ROWS, ROWS), dim)
        end = jnp.int32(0)
        clip = jnp.zeros((ROWS, ROWS), jnp.int32)
        for n in range(16):
            end = end + counts[0, n]
            clip = clip + jnp.where(frame >= end, 1, 0)
        return clip

    same = clip_of(0) == clip_of(1)

    z_wait(0, zc)
    rback[...] = rows_of(zc)
    z_wait(1, zt)
    total[...] = jnp.concatenate([zt[i].astype(F32) for i in range(16)], axis=0)
    for n in range(3):
        hid_p[:, columns(n)] = (total[:, columns(n)] + dot(rback[...], weights(3 * n))).astype(BF16)
    stage(1, 3)
    stage(2, 2)
    normed[...] = layer_norm(hid_p[...].astype(F32))
    for n in range(3):
        hid_f[:, columns(n)] = (tok[:, columns(n)].astype(F32) + dot(ctx[...], weights(3 * n))).astype(BF16)

    stage(1, 4)

    def project(part, first, count=3):
        product = dot(normed[...], weights(9 + 9 * part + first, count))
        qkv[part, :, LANES * first : LANES * (first + count)] = product.astype(BF16)

    def return_z(n, tiles, src, dst):
        for i, t in enumerate(tiles):
            tile = temporal.tile(t)
            for r in range(16):
                src[r, :, i * LANES : (i + 1) * LANES] = tile[8 * r : 8 * r + 8].astype(BF16)
        z_exchange(n, src, dst)

    def return_x(n, landed, src, dst):
        z_wait(n, landed)
        moved = swap_rows(rows_of(landed), 16)
        for i in range(8):
            src[i] = moved[16 * i : 16 * i + 16].astype(BF16)
        x_exchange(n, src, dst)

    for part, first in ((0, 0), (1, 0), (2, 0), (0, 3), (1, 3), (2, 3), (0, 6)):
        project(part, first)
    project(1, 6, 2)
    temporal = Attention(qkv.at[0], qkv.at[1], qkv.at[2], same)
    temporal.heads(0, 10)
    return_z(2, range(5), zs_a, zr_a)
    stage(2, 3)
    stage(2, 4)
    project(1, 8, 1)
    project(2, 6)
    temporal.heads(10, 16)
    return_z(3, range(5, 9), zs_b, zr_b)
    return_x(2, zr_a, xs_a, xr_a)
    return_x(3, zr_b, xs_b, xr_b)

    x_wait(2, xr_a)
    rback[:, :EARLY] = xr_a[...].reshape(ROWS, EARLY)
    for n in range(3):
        product = dot(rback[:, :EARLY], weights(36 + 3 * n, 3, slice(0, EARLY)))
        total[:, columns(n)] = hid_f[:, columns(n)].astype(F32) + product
    x_wait(3, xr_b)
    rback[:, EARLY:] = xr_b[...].reshape(ROWS, WIDTH - EARLY)
    for n in range(3):
        product = dot(rback[:, EARLY:], weights(36 + 3 * n, 3, slice(EARLY, WIDTH)))
        out[:, columns(n)] = (total[:, columns(n)] + product).astype(BF16)

    for copy in sends:
        copy.wait_send()
    for on, copy in maybe:
        pl.when(on)(copy.wait_send)


def shards(
    tokens,
    spatial_query,
    spatial_key,
    spatial_value,
    frame_counts,
    w_spatial_out,
    w_temporal_qkv,
    w_temporal_out,
):
    def padded(array, lanes):
        return jnp.pad(array, ((0, 16 - array.shape[0]), (0, lanes - array.shape[1])))

    wraw = jnp.concatenate(
        [padded(w_spatial_out, 384), padded(w_temporal_qkv, 896), padded(w_temporal_out, 512)], axis=1
    )
    flat = (ROWS, WIDTH)
    vmem = pl.BlockSpec(memory_space=pltpu.VMEM)
    late = WIDTH - EARLY
    dma = pltpu.SemaphoreType.DMA
    result = pl.pallas_call(
        kernel,
        out_shape=jax.ShapeDtypeStruct(flat, BF16),
        in_specs=[pl.BlockSpec(memory_space=pltpu.SMEM)] + [pl.BlockSpec(memory_space=pl.ANY)] * 5,
        out_specs=vmem,
        scratch_shapes=[
            *[pltpu.VMEM(flat, BF16)] * 4,
            pltpu.VMEM((4, 16, RAW), BF16),
            pltpu.VMEM((STEPS, 4, 3 * LANES, LANES), BF16),
            pltpu.VMEM((4, STEPS, 16, LANES), BF16),
            pltpu.VMEM((16, STEPS, 16, LANES), BF16),
            pltpu.VMEM((STEPS, 4, 4, 8, PAIR, LANES), BF16),
            pltpu.VMEM(flat, BF16),
            pltpu.VMEM((8, 16, WIDTH), BF16),
            pltpu.VMEM((8, 16, WIDTH), BF16),
            *[pltpu.VMEM((16, 8, WIDTH), BF16)] * 4,
            pltpu.VMEM(flat, BF16),
            pltpu.VMEM(flat, BF16),
            pltpu.VMEM(flat, BF16),
            pltpu.VMEM((3,) + flat, BF16),
            pltpu.VMEM((16, 8, EARLY), BF16),
            pltpu.VMEM((16, 8, late), BF16),
            pltpu.VMEM((16, 8, EARLY), BF16),
            pltpu.VMEM((16, 8, late), BF16),
            pltpu.VMEM((8, 16, EARLY), BF16),
            pltpu.VMEM((8, 16, late), BF16),
            pltpu.VMEM((8, 16, EARLY), BF16),
            pltpu.VMEM((8, 16, late), BF16),
            pltpu.VMEM(flat, BF16),
            pltpu.VMEM(flat, F32),
            dma((5,)),
            dma((4,)), dma((4,)),
            dma((8,)), dma((16,)),
            dma((STEPS, 2, 4)), dma((STEPS, 8)),
            dma((STEPS, 2, 18)), dma((STEPS, 2, 18)),
            dma((4, 16)), dma((4, 16)),
            dma((4, 8)), dma((4, 8)),
        ],
        compiler_params=pltpu.CompilerParams(
            collective_id=0, has_side_effects=True, vmem_limit_bytes=50 * 2**20
        ),
    )(
        frame_counts,
        tokens.reshape(flat),
        spatial_query.reshape(flat),
        spatial_key.reshape(flat),
        spatial_value.reshape(flat),
        wraw,
    )
    return result.reshape(tokens.shape)


def solution(mesh):
    placed = (
        P("batch", "seq", None, None),
        P("batch", "seq", None, None),
        P("batch", "seq", None, None),
        P("batch", "seq", None, None),
        P("batch", None),
        P("seq", "batch"),
        P("seq", "batch"),
        P("seq", "batch"),
    )
    return jax.shard_map(
        shards, mesh=mesh, in_specs=placed, out_specs=P("batch", "seq", None, None), check_vma=False
    )
```

time: 135 us -> 129 us (0.956)
  Pallas kernels: 130 us -> 124 us
    pallas_call x1, Pallas kernels: 130 us -> 124 us  [shards(): pl.pallas_call(kernel, out_shape=jax.ShapeDtypeStruct(flat, BF16), in_spe...]
where the time goes in v2:
time: 129 us
  Pallas kernels  124 us (96%)
  local copies, waits for them, and re-layouts  4.56 us (4%)
    pallas_call x1, Pallas kernels, shards(): pl.pallas_call(kernel, out_shape=jax.ShapeDtypeStruct(flat, BF16), in_spe...  124 us
    unnamed x11, local copies, waits for them, and re-layouts  4.56 us

profile of v2, /device:TPU:1, one launch (start us, length us, event | category | flops | bytes accessed | tf_op | source)
XLA Modules:
  0.0 129.2 jit_solution(17812298741251175323)
XLA Ops:
  0.0 0.0 copy-start.4
  0.0 0.8 fusion.5.wraw
  0.8 0.0 copy-done.4
  0.8 0.0 copy-start
  0.8 1.0 copy-done
  1.8 0.0 copy-start.1
  1.8 1.0 copy-done.1
  2.7 0.0 copy-start.2
  2.7 1.0 copy-done.2
  3.7 0.0 copy-start.3
  3.7 1.0 copy-done.3
  4.7 123.8 %shard_map.82 = bf16[128,1152]{1,0:T(8,128)(2,1)S(1)} custom-call(s32[1,16]{1,0:T(1,128)S(1)} %copy-done.4, bf16[128,1152]{1,0:T(8,128)(2,1)S(1)} %bitcast.6, bf16[128,1152]{1,0:T(8,128)(2,1)S(1)} %bitcast.7, bf16[128,1152]{1,0:T(8,128)(2,1)S(1)} %bitcast.8, bf16[128,1152]{1,0:T(8,128)(2,1)S(1)} %bitcast.9, bf16[16,1792]{1,0:T(8,128)(2,1)S(1)} %fusion.5.wraw), custom_call_target="tpu_custom_call" | custom-call | tf_op jit(solution)/shard_map/pallas_call | solution.py:491
  128.5 0.7 copy.10
Async XLA Ops:
  0.0 0.8 copy-start.4
  0.8 1.0 copy-start
  1.8 1.0 copy-start.1
  2.7 1.0 copy-start.2
  3.7 1.0 copy-start.3

commit v3 on v2

--- a/solution.py
+++ b/solution.py
@@ -19,11 +19,11 @@
 RAW = 1792
 STEPS = 3
 PAIR = 144
-EARLY = 640
+CHUNK = 384
 
 ORDER = list(range(9)) + [9, 10, 11, 18, 19, 20, 27]
-ORDER += [28, 29, 12, 13, 14, 21, 22, 23, 30, 31, 32, 15, 16, 17, 24, 25]
-ORDER += [26, 33, 34, 35] + list(range(36, 45)) + [44, 44, 44]
+ORDER += [28, 29, 12, 13, 14, 15, 21, 22, 23, 24, 30, 31, 32, 33, 16, 25]
+ORDER += [17, 26, 34, 35] + list(range(36, 45)) + [44, 44, 44]
 
 
 def dot(left, right):
@@ -78,7 +78,7 @@
 def kernel(
     counts, tok_in, sq_in, sk_in, sv_in, wraw, out,
     tok, sq, sk, sv, raw, picks, piece, gat, wts, ctx, xt, xc_in, zst, zsc, zt, zc,
-    hid_f, hid_p, normed, qkv, zs_a, zs_b, zr_a, zr_b, xs_a, xs_b, xr_a, xr_b, rback, total,
+    hid_f, hid_p, normed, qkv, zs, zr, xs, xr, rback, total,
     in_s, y_s, y_r, g_s, g_r, p_s, p_r, w_s, w_r, z_s, z_r, x_s, x_r,
 ):
     me = lax.axis_index("seq")
@@ -136,6 +136,51 @@
     ]
     for load in loads:
         load.start()
+    loads[0].wait()
+    pl.semaphore_wait(barrier, len(peers))
+
+    for d in (1, 2, 3):
+        send(raw.at[y], raw.at[y], y_s.at[d], y_r.at[y], at(z, xc, ring(y, d, 4)))
+
+    def z_exchange(n, src, dst):
+        for d in range(1, 16):
+            to = ring(z, d, 16)
+            send(src.at[to], dst.at[z], z_s.at[n, d], z_r.at[n, z], at(to, xc, y))
+        dst[z] = src[z]
+
+    def z_wait(n, dst):
+        for d in range(1, 16):
+            source = ring(z, d, 16)
+            arrived(dst.at[source], z_s.at[n, d], z_r.at[n, source])
+
+    def block(src, index):
+        if len(src.shape) == 3:
+            return src.at[index]
+        return src.at[pl.ds(pl.multiple_of(index * 16, 16), 16)]
+
+    def x_exchange(n, src, dst):
+        for d in range(1, 8):
+            to = ring(xc, d, 8)
+            send(block(src, to), dst.at[xc], x_s.at[n, d], x_r.at[n, xc], at(z, to, y))
+        dst[xc] = block(src, xc)[...]
+
+    def x_wait(n, dst):
+        for d in range(1, 8):
+            source = ring(xc, d, 8)
+            arrived(dst.at[source], x_s.at[n, d], x_r.at[n, source])
+
+    def rows_of(ref):
+        return jnp.concatenate([ref[i].astype(F32) for i in range(16)], axis=0).astype(BF16)
+
+    def swap_rows(left, inner):
+        outer = ROWS // inner
+        i, k = iota((ROWS, ROWS), 0), iota((ROWS, ROWS), 1)
+        pick = k == lax.rem(i, inner) * outer + lax.div(i, inner)
+        return dot(jnp.where(pick, 1.0, 0.0).astype(BF16), left)
+
+    loads[1].wait()
+    x_exchange(1, tok, xt)
+
     places = []
     row, col = iota((3 * LANES, LANES), 0), iota((3 * LANES, LANES), 1)
     for j in range(STEPS):
@@ -143,72 +188,19 @@
             tile = sum(jnp.where(y == i, ORDER[16 * j + 4 * x2 + i], 0) for i in range(4))
             second = jnp.where(tile >= 9, 1, 0)
             third = jnp.where(tile >= 36, 1, 0)
-            block = 288 + 576 * (second - third)
+            held = 288 + 576 * (second - third)
             lanes = 384 * second + 896 * third
             begin = LANES * (tile - 9 * second - 27 * third)
             y1 = jnp.where(second - third == 1, lax.div(begin, 864), lax.div(begin, 288))
             y2 = jnp.minimum(y1 + 1, 3)
-            inside = begin - y1 * block
+            inside = begin - y1 * held
             skip = lax.rem(inside, LANES)
-            first = jnp.minimum(block - inside, LANES)
+            first = jnp.minimum(held - inside, LANES)
             near = (row == col + skip) & (col < first)
             far = (row == col - first + 2 * LANES) & (col >= first)
             picks[j, x2] = jnp.where(near | far, 1.0, 0.0).astype(BF16)
             places.append((j, x2, y1, pl.multiple_of(lanes + inside - skip, LANES), y2, pl.multiple_of(lanes, LANES)))
 
-    for load in loads[2:]:
-        load.wait()
-    spatial = Attention(sq, sk, sv, None)
-    spatial.heads(0, HEADS)
-    for i in range(9):
-        ctx[:, i * LANES : (i + 1) * LANES] = spatial.tile(i).astype(BF16)
-    loads[0].wait()
-    loads[1].wait()
-
-    pl.semaphore_wait(barrier, len(peers))
-
-    for d in (1, 2, 3):
-        send(raw.at[y], raw.at[y], y_s.at[d], y_r.at[y], at(z, xc, ring(y, d, 4)))
-
-    def z_exchange(n, src, dst):
-        for d in range(1, 16):
-            to = ring(z, d, 16)
-            send(src.at[to], dst.at[z], z_s.at[n, d], z_r.at[n, z], at(to, xc, y))
-        dst[z] = src[z]
-
-    def z_wait(n, dst):
-        for d in range(1, 16):
-            source = ring(z, d, 16)
-            arrived(dst.at[source], z_s.at[n, d], z_r.at[n, source])
-
-    def block(src, index):
-        if len(src.shape) == 3:
-            return src.at[index]
-        return src.at[pl.ds(pl.multiple_of(index * 16, 16), 16)]
-
-    def x_exchange(n, src, dst):
-        for d in range(1, 8):
-            to = ring(xc, d, 8)
-            send(block(src, to), dst.at[xc], x_s.at[n, d], x_r.at[n, xc], at(z, to, y))
-        dst[xc] = block(src, xc)[...]
-
-    def x_wait(n, dst):
-        for d in range(1, 8):
-            source = ring(xc, d, 8)
-            arrived(dst.at[source], x_s.at[n, d], x_r.at[n, source])
-
-    def rows_of(ref):
-        return jnp.concatenate([ref[i].astype(F32) for i in range(16)], axis=0).astype(BF16)
-
-    def swap_rows(left, inner):
-        outer = ROWS // inner
-        i, k = iota((ROWS, ROWS), 0), iota((ROWS, ROWS), 1)
-        pick = k == lax.rem(i, inner) * outer + lax.div(i, inner)
-        return dot(jnp.where(pick, 1.0, 0.0).astype(BF16), left)
-
-    x_exchange(0, ctx, xc_in)
-    x_exchange(1, tok, xt)
-
     for d in (1, 2, 3):
         source = ring(y, d, 4)
         arrived(raw.at[source], y_s.at[d], y_r.at[source])
@@ -217,6 +209,13 @@
         left = raw[y1, :, pl.ds(start1, 2 * LANES)]
         right = raw[y2, :, pl.ds(start2, LANES)]
         piece[x2, j] = dot(jnp.concatenate([left, right], axis=1), picks[j, x2]).astype(BF16)
+
+    def to_z(n, landed, src, dst):
+        x_wait(n, landed)
+        moved = swap_rows(landed[...].reshape(ROWS, WIDTH), 8)
+        for i in range(16):
+            src[i] = moved[8 * i : 8 * i + 8].astype(BF16)
+        z_exchange(n, src, dst)
 
     source = 8 * zpar + xc
     for zo in (0, 1):
@@ -233,6 +232,11 @@
                 send_if(jnp.logical_not(active), piece.at[x2], gat.at[source], sem, g_r.at[source], where)
             else:
                 send(piece.at[x2], gat.at[source], sem, g_r.at[source], where)
+
+    for load in loads[2:]:
+        load.wait()
+    spatial = Attention(sq, sk, sv, None)
+    spatial.heads(0, 4)
 
     @pl.when(active)
     def _():
@@ -263,20 +267,16 @@
             to = ring(z, hop * way, 16)
             send_if(on, spot, spot, p_s.at[j, min(m, 1), hop - 1], p_r.at[j, block], at(to, xc, y))
 
-    def to_z(n, landed, src, dst):
-        x_wait(n, landed)
-        moved = swap_rows(landed[...].reshape(ROWS, WIDTH), 8)
-        for i in range(16):
-            src[i] = moved[8 * i : 8 * i + 8].astype(BF16)
-        z_exchange(n, src, dst)
-
-    for j in range(STEPS):
-        along(j, 0, (4, 3, 2, 1))
-    to_z(0, xc_in, zsc, zc)
+    along(0, 0, (4, 3, 2, 1))
+    spatial.heads(4, 8)
     along(0, 2, (3, 2, 1))
     to_z(1, xt, zst, zt)
-    along(1, 2, (3, 2, 1))
-    along(2, 2, (3, 2, 1))
+    along(1, 0, (4, 3, 2, 1))
+    along(2, 0, (4, 3, 2, 1))
+    spatial.heads(8, HEADS)
+    for i in range(9):
+        ctx[:, i * LANES : (i + 1) * LANES] = spatial.tile(i).astype(BF16)
+    x_exchange(0, ctx, xc_in)
 
     up, down = (lambda v: ring(v, 1, 4)), (lambda v: ring(v, -1, 4))
     far = lambda v: ring(v, 2, 4)
@@ -383,13 +383,15 @@
         return slice(384 * n, 384 * n + 384)
 
     stage(0, 0)
+    along(1, 2, (3, 2, 1))
+    along(2, 2, (3, 2, 1))
+    to_z(0, xc_in, zsc, zc)
+    stage(0, 1)
     stage(1, 0)
-    stage(0, 1)
+    stage(0, 2)
+    stage(1, 1)
+    stage(0, 3)
     stage(2, 0)
-    stage(1, 1)
-    stage(0, 2)
-    stage(2, 1)
-    stage(0, 3)
     stage(1, 2)
     stage(0, 4)
 
@@ -411,56 +413,61 @@
     for n in range(3):
         hid_p[:, columns(n)] = (total[:, columns(n)] + dot(rback[...], weights(3 * n))).astype(BF16)
     stage(1, 3)
-    stage(2, 2)
+    stage(2, 1)
     normed[...] = layer_norm(hid_p[...].astype(F32))
-    for n in range(3):
-        hid_f[:, columns(n)] = (tok[:, columns(n)].astype(F32) + dot(ctx[...], weights(3 * n))).astype(BF16)
-
     stage(1, 4)
-
     def project(part, first, count=3):
         product = dot(normed[...], weights(9 + 9 * part + first, count))
         qkv[part, :, LANES * first : LANES * (first + count)] = product.astype(BF16)
 
-    def return_z(n, tiles, src, dst):
-        for i, t in enumerate(tiles):
-            tile = temporal.tile(t)
+    def return_z(n):
+        for i in range(3):
+            tile = temporal.tile(3 * n + i)
             for r in range(16):
-                src[r, :, i * LANES : (i + 1) * LANES] = tile[8 * r : 8 * r + 8].astype(BF16)
-        z_exchange(n, src, dst)
-
-    def return_x(n, landed, src, dst):
-        z_wait(n, landed)
-        moved = swap_rows(rows_of(landed), 16)
+                zs[n, r, :, i * LANES : (i + 1) * LANES] = tile[8 * r : 8 * r + 8].astype(BF16)
+        z_exchange(2 + n, zs.at[n], zr.at[n])
+
+    def return_x(n):
+        z_wait(2 + n, zr.at[n])
+        moved = swap_rows(rows_of(zr.at[n]), 16)
         for i in range(8):
-            src[i] = moved[16 * i : 16 * i + 16].astype(BF16)
-        x_exchange(n, src, dst)
-
-    for part, first in ((0, 0), (1, 0), (2, 0), (0, 3), (1, 3), (2, 3), (0, 6)):
-        project(part, first)
-    project(1, 6, 2)
+            xs[n, i] = moved[16 * i : 16 * i + 16].astype(BF16)
+        x_exchange(2 + n, xs.at[n], xr.at[n])
+
+    for part in range(3):
+        project(part, 0)
+        project(part, 3)
+        project(part, 6, 1 if part == 2 else 2)
     temporal = Attention(qkv.at[0], qkv.at[1], qkv.at[2], same)
-    temporal.heads(0, 10)
-    return_z(2, range(5), zs_a, zr_a)
+    temporal.heads(0, 6)
+    return_z(0)
+    stage(2, 2)
+    temporal.heads(6, 11)
+    return_z(1)
+    for n in range(3):
+        hid_f[:, columns(n)] = (tok[:, columns(n)].astype(F32) + dot(ctx[...], weights(3 * n))).astype(BF16)
     stage(2, 3)
     stage(2, 4)
+    project(0, 8, 1)
     project(1, 8, 1)
-    project(2, 6)
-    temporal.heads(10, 16)
-    return_z(3, range(5, 9), zs_b, zr_b)
-    return_x(2, zr_a, xs_a, xr_a)
-    return_x(3, zr_b, xs_b, xr_b)
-
-    x_wait(2, xr_a)
-    rback[:, :EARLY] = xr_a[...].reshape(ROWS, EARLY)
-    for n in range(3):
-        product = dot(rback[:, :EARLY], weights(36 + 3 * n, 3, slice(0, EARLY)))
-        total[:, columns(n)] = hid_f[:, columns(n)].astype(F32) + product
-    x_wait(3, xr_b)
-    rback[:, EARLY:] = xr_b[...].reshape(ROWS, WIDTH - EARLY)
-    for n in range(3):
-        product = dot(rback[:, EARLY:], weights(36 + 3 * n, 3, slice(EARLY, WIDTH)))
-        out[:, columns(n)] = (total[:, columns(n)] + product).astype(BF16)
+    project(2, 7, 2)
+    temporal.heads(11, HEADS)
+    return_z(2)
+    return_x(0)
+    return_x(1)
+    return_x(2)
+
+    for part in range(3):
+        x_wait(2 + part, xr.at[part])
+        rback[:, :CHUNK] = xr[part].reshape(ROWS, CHUNK)
+        depth = slice(part * CHUNK, part * CHUNK + CHUNK)
+        for n in range(3):
+            before = hid_f[:, columns(n)].astype(F32) if part == 0 else total[:, columns(n)]
+            after = before + dot(rback[:, :CHUNK], weights(36 + 3 * n, 3, depth))
+            if part < 2:
+                total[:, columns(n)] = after
+            else:
+                out[:, columns(n)] = after.astype(BF16)
 
     for copy in sends:
         copy.wait_send()
@@ -486,7 +493,6 @@
     )
     flat = (ROWS, WIDTH)
     vmem = pl.BlockSpec(memory_space=pltpu.VMEM)
-    late = WIDTH - EARLY
     dma = pltpu.SemaphoreType.DMA
     result = pl.pallas_call(
         kernel,
@@ -508,23 +514,17 @@
             pltpu.VMEM(flat, BF16),
             pltpu.VMEM(flat, BF16),
             pltpu.VMEM((3,) + flat, BF16),
-            pltpu.VMEM((16, 8, EARLY), BF16),
-            pltpu.VMEM((16, 8, late), BF16),
-            pltpu.VMEM((16, 8, EARLY), BF16),
-            pltpu.VMEM((16, 8, late), BF16),
-            pltpu.VMEM((8, 16, EARLY), BF16),
-            pltpu.VMEM((8, 16, late), BF16),
-            pltpu.VMEM((8, 16, EARLY), BF16),
-            pltpu.VMEM((8, 16, late), BF16),
+            *[pltpu.VMEM((3, 16, 8, CHUNK), BF16)] * 2,
+            *[pltpu.VMEM((3, 8, 16, CHUNK), BF16)] * 2,
             pltpu.VMEM(flat, BF16),
             pltpu.VMEM(flat, F32),
             dma((5,)),
             dma((4,)), dma((4,)),
             dma((8,)), dma((16,)),
-            dma((STEPS, 2, 4)), dma((STEPS, 8)),
+            dma((STEPS, 2, 7)), dma((STEPS, 8)),
             dma((STEPS, 2, 18)), dma((STEPS, 2, 18)),
-            dma((4, 16)), dma((4, 16)),
-            dma((4, 8)), dma((4, 8)),
+            dma((5, 16)), dma((5, 16)),
+            dma((5, 8)), dma((5, 8)),
         ],
         compiler_params=pltpu.CompilerParams(
             collective_id=0, has_side_effects=True, vmem_limit_bytes=50 * 2**20

time: 129 us -> 118 us (0.915)
  Pallas kernels: 124 us -> 113 us
    pallas_call x1, Pallas kernels: 124 us -> 113 us  [shards(): pl.pallas_call(kernel, out_shape=jax.ShapeDtypeStruct(flat, BF16), in_spe...]
where the time goes in v3:
time: 118 us
  Pallas kernels  113 us (96%)
  local copies, waits for them, and re-layouts  4.56 us (4%)
    pallas_call x1, Pallas kernels, shards(): pl.pallas_call(kernel, out_shape=jax.ShapeDtypeStruct(flat, BF16), in_spe...  113 us
    unnamed x11, local copies, waits for them, and re-layouts  4.56 us

profile of v3, /device:TPU:1, one launch (start us, length us, event | category | flops | bytes accessed | tf_op | source)
XLA Modules:
  0.0 117.9 jit_solution(2027307288801347375)
XLA Ops:
  0.0 0.0 copy-start.4
  0.0 0.8 fusion.5.wraw
  0.8 0.0 copy-done.4
  0.8 0.0 copy-start
  0.8 1.0 copy-done
  1.8 0.0 copy-start.1
  1.8 1.0 copy-done.1
  2.7 0.0 copy-start.2
  2.7 1.0 copy-done.2
  3.7 0.0 copy-start.3
  3.7 1.0 copy-done.3
  4.7 112.5 %shard_map.82 = bf16[128,1152]{1,0:T(8,128)(2,1)S(1)} custom-call(s32[1,16]{1,0:T(1,128)S(1)} %copy-done.4, bf16[128,1152]{1,0:T(8,128)(2,1)S(1)} %bitcast.6, bf16[128,1152]{1,0:T(8,128)(2,1)S(1)} %bitcast.7, bf16[128,1152]{1,0:T(8,128)(2,1)S(1)} %bitcast.8, bf16[128,1152]{1,0:T(8,128)(2,1)S(1)} %bitcast.9, bf16[16,1792]{1,0:T(8,128)(2,1)S(1)} %fusion.5.wraw), custom_call_target="tpu_custom_call" | custom-call | tf_op jit(solution)/shard_map/pallas_call | solution.py:497
  117.2 0.7 copy.10
Async XLA Ops:
  0.0 0.8 copy-start.4
  0.8 1.0 copy-start
  1.8 1.0 copy-start.1
  2.7 1.0 copy-start.2
  3.7 1.0 copy-start.3

commit v4 on v3

--- a/solution.py
+++ b/solution.py
@@ -453,9 +453,14 @@
     project(2, 7, 2)
     temporal.heads(11, HEADS)
     return_z(2)
+    settled = len(sends)
     return_x(0)
     return_x(1)
     return_x(2)
+    for copy in sends[:settled]:
+        copy.wait_send()
+    for on, copy in maybe:
+        pl.when(on)(copy.wait_send)
 
     for part in range(3):
         x_wait(2 + part, xr.at[part])
@@ -469,10 +474,8 @@
             else:
                 out[:, columns(n)] = after.astype(BF16)
 
-    for copy in sends:
+    for copy in sends[settled:]:
         copy.wait_send()
-    for on, copy in maybe:
-        pl.when(on)(copy.wait_send)
 
 
 def shards(

time: 118 us -> 118 us (level)
  no operation moved by 1% of the time
where the time goes in v4:
time: 118 us
  Pallas kernels  112 us (95%)
  local copies, waits for them, and re-layouts  4.56 us (4%)
    pallas_call x1, Pallas kernels, shards(): pl.pallas_call(kernel, out_shape=jax.ShapeDtypeStruct(flat, BF16), in_spe...  112 us
    unnamed x11, local copies, waits for them, and re-layouts  4.56 us

profile of v4, /device:TPU:1, one launch (start us, length us, event | category | flops | bytes accessed | tf_op | source)
XLA Modules:
  0.0 117.6 jit_solution(14947783028302511725)
XLA Ops:
  0.0 0.0 copy-start.4
  0.0 0.8 fusion.5.wraw
  0.8 0.0 copy-done.4
  0.8 0.0 copy-start
  0.8 1.0 copy-done
  1.8 0.0 copy-start.1
  1.8 1.0 copy-done.1
  2.7 0.0 copy-start.2
  2.7 1.0 copy-done.2
  3.7 0.0 copy-start.3
  3.7 1.0 copy-done.3
  4.7 112.2 %shard_map.82 = bf16[128,1152]{1,0:T(8,128)(2,1)S(1)} custom-call(s32[1,16]{1,0:T(1,128)S(1)} %copy-done.4, bf16[128,1152]{1,0:T(8,128)(2,1)S(1)} %bitcast.6, bf16[128,1152]{1,0:T(8,128)(2,1)S(1)} %bitcast.7, bf16[128,1152]{1,0:T(8,128)(2,1)S(1)} %bitcast.8, bf16[128,1152]{1,0:T(8,128)(2,1)S(1)} %bitcast.9, bf16[16,1792]{1,0:T(8,128)(2,1)S(1)} %fusion.5.wraw), custom_call_target="tpu_custom_call" | custom-call | tf_op jit(solution)/shard_map/pallas_call | solution.py:500
  116.9 0.7 copy.10
Async XLA Ops:
  0.0 0.8 copy-start.4
  0.8 1.0 copy-start
  1.8 1.0 copy-start.1
  2.7 1.0 copy-start.2
  3.7 1.0 copy-start.3
